TPU v7x, 512 devices: a whole 4x8x8 slice. The times are simulated.
512 devices in a mesh: ctx: 64 (over y_hi, z, core), head: 8 (over y_lo, x).
Axes of the slice: x: 4, y: 8 (y_hi: 4, y_lo: 2; y = y_hi * 2 + y_lo), z: 8, core: 2. Of those that a mesh axis runs over, the one named last changes fastest.
Arguments:
- queries: bfloat16 [256, 16384], P('ctx', 'head'), may hold values from -7 to 7
- grad_out: bfloat16 [256, 16384], P('ctx', 'head'), may hold values from -384 to 384
- outputs: bfloat16 [256, 16384], P('ctx', 'head'), may hold values from -6 to 6
- lse_self: float32 [256, 128], P('ctx', 'head'), may hold values from 0 to 20
- prompt_keys: bfloat16 [16384, 1024], P(('ctx', 'head')), may hold values from -11 to 11
- prompt_values: bfloat16 [16384, 1024], P(('ctx', 'head')), may hold values from -6 to 6
- resp_len: int32 [4], replicated, may hold values from 16 to 64, as said below
- prompt_end: int32 [4], replicated, may hold values from 8192 to 16384, as said below
Outputs:
- query_grad: bfloat16 [256, 16384], P('ctx', 'head')
- prompt_key_grad: bfloat16 [16384, 1024], P(('ctx', 'head'))
- prompt_value_grad: bfloat16 [16384, 1024], P(('ctx', 'head'))
Inputs may be any that keep to these rules, and one draw needn't show every extreme that they name: `resp_len`: at least one response has all 64 rows live. `prompt_end`: at least one response sees the whole prompt.
All inputs are finite; a program needn't handle non-finite values.
Results may differ from a plain program's by a relative error of at most 0.013.
Values may be sent and summed in bfloat16 or wider, within the bound.
A program may use at most 64 MiB of HBM per device.

v0:
```python
import math

import jax
import jax.numpy as jnp
from jax import lax
from jax.sharding import PartitionSpec as P

DH = 128
RESP_LEN = 64


MASKED_SCORE = -1e30


def combined_all(x, axis, combine):
    everything = jax.tree.map(lambda part: lax.all_gather(part, axis), x)
    initial = jax.tree.map(lambda part: part[0], everything)

    def hop(k, so_far):
        return combine(so_far, jax.tree.map(lambda part: part[k], everything))

    return lax.fori_loop(1, lax.axis_size(axis), hop, initial)


def combine_rows(first_part, second_part):
    higher = jnp.maximum(first_part[0], second_part[0])
    merged_total = first_part[1] * jnp.exp(first_part[0] - higher) + second_part[1] * jnp.exp(
        second_part[0] - higher
    )
    return (higher, merged_total)


def shards(queries, grad_out, outputs, lse_self, prompt_keys, prompt_values, resp_len, prompt_end):
    key_local, value_local = (
        lax.all_to_all(prompt_keys, "head", split_axis=1, concat_axis=0, tiled=True),
        lax.all_to_all(prompt_values, "head", split_axis=1, concat_axis=0, tiled=True),
    )
    own_count = queries.shape[0]
    head_count = queries.shape[1] // DH
    group_count = key_local.shape[1] // DH
    per_group = head_count // group_count
    head_block = math.gcd(per_group, 2)
    block_count = head_count // head_block
    key_count = key_local.shape[0]
    ctx_index = lax.axis_index("ctx")
    own_start = ctx_index * own_count
    score_scale = DH ** (-0.5)
    query_all, grad_all, output_all = (
        lax.all_gather(queries, "ctx", axis=0, tiled=True),
        lax.all_gather(grad_out, "ctx", axis=0, tiled=True),
        lax.all_gather(outputs, "ctx", axis=0, tiled=True),
    )
    row_count = query_all.shape[0]
    row_dots = jnp.einsum(
        "rhd,rhd->rh",
        grad_all.reshape(row_count, head_count, DH),
        output_all.reshape(row_count, head_count, DH),
        preferred_element_type=jnp.float32,
    )
    row_ids = jnp.arange(row_count, dtype=jnp.int32)
    resp_ids = jnp.arange(resp_len.shape[0], dtype=jnp.int32)
    member = (row_ids // RESP_LEN)[:, None] == resp_ids[None, :]
    length_row = jnp.sum(jnp.where(member, resp_len[None, :], 0), axis=1)
    end_row = jnp.sum(jnp.where(member, prompt_end[None, :], 0), axis=1)
    live_rows = (row_ids % RESP_LEN < length_row).astype(jnp.float32)
    key_position = ctx_index * key_count + jnp.arange(key_count, dtype=jnp.int32)
    visible = key_position[None, :] < end_row[:, None]

    def block_scores(block_index):
        head_first = block_index * head_block
        query_block = lax.dynamic_slice_in_dim(
            query_all, head_first * DH, head_block * DH, 1
        ).reshape(row_count, head_block, DH)
        scores = (
            jnp.einsum("rbd,kd->brk", query_block, key_local, preferred_element_type=jnp.float32)
            * score_scale
        )
        return (head_first, query_block, key_local, scores)

    def stat_step(unused, block_index):
        head_first, query_block, key_group, scores = block_scores(block_index)
        scores = jnp.where(visible[None], scores, MASKED_SCORE)
        block_peak = jnp.max(scores, axis=2)
        block_total = jnp.sum(
            jnp.where(visible[None], jnp.exp(scores - block_peak[:, :, None]), 0.0), axis=2
        )
        return (unused, (block_peak, block_total))

    _, (peaks, totals) = lax.scan(
        stat_step, jnp.zeros((), jnp.float32), jnp.arange(block_count, dtype=jnp.int32)
    )
    row_peak = peaks.reshape(head_count, row_count).T
    row_total = totals.reshape(head_count, row_count).T
    own_peak = lax.dynamic_slice_in_dim(row_peak, own_start, own_count, 0)
    own_total = lax.dynamic_slice_in_dim(row_total, own_start, own_count, 0)
    own_peak, own_total = combine_rows((own_peak, own_total), (lse_self, jnp.ones_like(lse_self)))
    row_peak = lax.dynamic_update_slice_in_dim(row_peak, own_peak, own_start, 0)
    row_total = lax.dynamic_update_slice_in_dim(row_total, own_total, own_start, 0)
    row_peak, row_total = combined_all((row_peak, row_total), "ctx", combine_rows)
    full_lse = row_peak + jnp.log(row_total)

    def grad_step(accums, block_index):
        key_acc, value_acc, query_acc = accums
        head_first, query_block, key_group, scores = block_scores(block_index)
        grad_block = lax.dynamic_slice_in_dim(
            grad_all, head_first * DH, head_block * DH, 1
        ).reshape(row_count, head_block, DH)
        lse_block = lax.dynamic_slice_in_dim(full_lse, head_first, head_block, 1).T
        dots_block = lax.dynamic_slice_in_dim(row_dots, head_first, head_block, 1).T
        prob = (
            jnp.where(visible[None], jnp.exp(scores - lse_block[:, :, None]), 0.0)
            * live_rows[None, :, None]
        )
        dprob = jnp.einsum(
            "rbd,kd->brk", grad_block, value_local, preferred_element_type=jnp.float32
        )
        dscore = (prob * (dprob - dots_block[:, :, None])).astype(jnp.bfloat16)
        value_add = jnp.einsum(
            "brk,rbd->kd", prob.astype(jnp.bfloat16), grad_block, preferred_element_type=jnp.float32
        )
        key_add = (
            jnp.einsum("brk,rbd->kd", dscore, query_block, preferred_element_type=jnp.float32)
            * score_scale
        )
        key_acc = key_acc + key_add
        value_acc = value_acc + value_add
        query_add = (
            jnp.einsum("brk,kd->rbd", dscore, key_group, preferred_element_type=jnp.float32)
            * score_scale
        )
        query_acc = lax.dynamic_update_slice_in_dim(
            query_acc, query_add.reshape(row_count, head_block * DH), head_first * DH, 1
        )
        return ((key_acc, value_acc, query_acc), None)

    zero_accums = (
        jnp.zeros((key_count, group_count * DH), jnp.float32),
        jnp.zeros((key_count, group_count * DH), jnp.float32),
        jnp.zeros((row_count, head_count * DH), jnp.float32),
    )
    (key_acc, value_acc, query_acc), _ = lax.scan(
        grad_step, zero_accums, jnp.arange(block_count, dtype=jnp.int32)
    )
    query_grad = lax.psum_scatter(query_acc, "ctx", scatter_dimension=0, tiled=True).astype(
        jnp.bfloat16
    )
    key_grad, value_grad = (
        lax.all_to_all(
            key_acc.astype(jnp.bfloat16), "head", split_axis=0, concat_axis=1, tiled=True
        ),
        lax.all_to_all(
            value_acc.astype(jnp.bfloat16), "head", split_axis=0, concat_axis=1, tiled=True
        ),
    )
    return (query_grad, key_grad, value_grad)


def solution(mesh):
    in_specs = (
        P("ctx", "head"),
        P("ctx", "head"),
        P("ctx", "head"),
        P("ctx", "head"),
        P(("ctx", "head"), None),
        P(("ctx", "head"), None),
        P(),
        P(),
    )
    out_specs = (P("ctx", "head"), P(("ctx", "head"), None), P(("ctx", "head"), None))
    return jax.shard_map(shards, mesh=mesh, in_specs=in_specs, out_specs=out_specs, check_vma=False)
```

profile of v0, /device:TPU:2, one launch (start us, length us, event | category | flops | bytes accessed | tf_op | source)
XLA Modules:
  0.0 861.7 jit_solution(11927188474583348325)
XLA Ops:
  9.3 9.2 %all-to-all-start = ((bf16[32,8,128]{2,0,1:T(8,128)(2,1)}), bf16[32,8,128]{2,0,1:T(8,128)(2,1)S(1)}, u32[]{:S(2)}, u32[]{:S(2)}) async-start(bf16[32,8,128]{2,0,1:T(8,128)(2,1)} %copy_bitcast_fusion.3), calls=%async_computation | async-start | bytes 131072 | tf_op jit(solution)/shard_map/all_to_all | solution.py:35
  20.1 79.1 %all-gather.13.cloned.1.call-done = bf16[64,4,2048]{2,1,0:T(4,128)(2,1)} async-done(((bf16[1,4,2048]{2,1,0:T(4,128)(2,1)}), bf16[64,4,2048]{2,1,0:T(4,128)(2,1)}) %all-gather.13.cloned.1.call-update) | async-done | bytes 1048592 | tf_op jit(solution)/shard_map/all_gather | solution.py:49
  99.1 1.3 reshape.95
  100.5 1.3 copy.173
  101.8 21.4 %while.50 = (s32[]{:T(128)}, f32[8,2,256]{2,1,0:T(2,128)S(1)}, f32[8,2,256]{2,1,0:T(2,128)S(1)}, s32[8]{0:T(128)S(1)}, bf16[256,2048]{0,1:T(8,128)(2,1)}, /*inde...) while((s32[]{:T(128)}, f32[8,2,256]{2,1,0:T(2,128)S(1)}, ...), condition=%wide.region_4.5_spmd.clone, body=%wide.region_1.4_spmd.clone.sunk | while | flops 34405380 | bytes 1720511 | solution.py:89
  126.1 4.8 all-to-all-start.1
  130.9 1.3 dynamic-slice.8
  133.6 48.3 %all-gather.17.cloned.1.call-done = bf16[64,4,2048]{2,1,0:T(4,128)(2,1)} async-done(((bf16[1,4,2048]{2,1,0:T(4,128)(2,1)}), bf16[64,4,2048]{2,1,0:T(4,128)(2,1)}) %all-gather.17.cloned.1.call-update) | async-done | bytes 1048592 | tf_op jit(solution)/shard_map/all_gather | solution.py:51
  181.9 1.7 reshape.93
  183.6 81.0 %all-gather.15.cloned.1.call-done = bf16[64,4,2048]{2,1,0:T(4,128)(2,1)} async-done(((bf16[1,4,2048]{2,1,0:T(4,128)(2,1)}), bf16[64,4,2048]{2,1,0:T(4,128)(2,1)}) %all-gather.15.cloned.1.call-update) | async-done | bytes 1048592 | tf_op jit(solution)/shard_map/all_gather | solution.py:50
  264.6 1.8 reshape.92
  266.5 1.3 fusion.24
  268.7 1.1 reshape.97
  269.8 78.0 %all-gather.9.cloned.1.call-done = f32[64,256,16]{1,2,0:T(8,128)} async-done(((f32[1,256,16]{1,2,0:T(8,128)}), f32[64,256,16]{1,2,0:T(8,128)}) %all-gather.9.cloned.1.call-update) | async-done | bytes 1048592 | tf_op jit(solution)/shard_map/all_gather | solution.py:16
  348.5 81.9 %all-gather.11.cloned.1.call-done = f32[64,256,16]{1,2,0:T(8,128)} async-done(((f32[1,256,16]{1,2,0:T(8,128)}), f32[64,256,16]{1,2,0:T(8,128)}) %all-gather.11.cloned.1.call-update) | async-done | bytes 1048592 | tf_op jit(solution)/shard_map/all_gather | solution.py:16
  431.1 49.0 %while.49 = (s32[]{:T(128)}, f32[256,16]{0,1:T(8,128)S(1)}, f32[256,16]{0,1:T(8,128)S(1)}, f32[64,256,16]{1,2,0:T(8,128)}, f32[64,256,16]{1,2,0:T(8,128)}, /*index=5*/s32[]{:T(128)}, s32[]{:T(128)}, s32[]{:T(128)}) while((s32[]{:T(128)}, f32[256,16]{0,1:T(8,128)S(1)}, f32[256,16]{0,1:T(8,128)S(1)}, f32[64,256,16]{1,2,0:T(8,128)}, ...), condition=%wide.region_6.7_spmd, body=%wide.region_5.6_spmd.sunk | while | flops 24581 | bytes 98427 | solution.py:22
  480.4 51.6 %while.51 = (s32[]{:T(128)}, f32[256,128]{1,0:T(8,128)S(1)}, f32[256,128]{1,0:T(8,128)S(1)}, f32[256,2048]{1,0:T(8,128)S(1)}, s32[8]{0:T(128)S(1)}, /*index=5*/b...) while((s32[]{:T(128)}, f32[256,128]{1,0:T(8,128)S(1)}, ...), condition=%wide.region_9.10_spmd.clone, body=%wide.region_8.9_spmd.clone.sunk | while | flops 169115648 | bytes 5848384 | solution.py:141
  491.5 1.1 fusion.74
  517.3 1.1 fusion.74
  532.0 302.7 %all-reduce.2 = bf16[256,2048]{1,0:T(8,128)(2,1)S(1)} all-reduce(f32[256,2048]{1,0:T(8,128)S(1)} %get-tuple-element.393), channel_id=2, replica_groups=mesh['ctx'=64,'head'=8] {'ctx'}, use_global_device_ids=true, to_apply=%region_10.11.clone | all-reduce | flops 524288 | bytes 3145728
  835.3 4.7 all-to-all-start.2
  841.3 3.6 all-to-all-done.2
  844.9 4.7 all-to-all-start.3
  850.3 4.3 all-to-all-done.3
  (272 shorter events, 114.8 us)
Async XLA Ops:
  7.2 1.5 copy-start
  7.2 92.0 %all-gather.13.cloned.1.call-start = ((), (), s32[]{:S(2)}) async-start(), calls=%async_computation.6 | async-start | bytes 1064960 | tf_op jit(solution)/shard_map/all_gather | solution.py:49
  7.9 174.0 %all-gather.17.cloned.1.call-start = ((), (), s32[]{:S(2)}) async-start(), calls=%async_computation.8 | async-start | bytes 1064960 | tf_op jit(solution)/shard_map/all_gather | solution.py:51
  9.3 92.5 %all-to-all-start = ((bf16[32,8,128]{2,0,1:T(8,128)(2,1)}), bf16[32,8,128]{2,0,1:T(8,128)(2,1)S(1)}, u32[]{:S(2)}, u32[]{:S(2)}) async-start(bf16[32,8,128]{2,0,1:T(8,128)(2,1)} %copy_bitcast_fusion.3), calls=%async_computation | async-start | bytes 131072 | tf_op jit(solution)/shard_map/all_to_all | solution.py:35
  18.5 246.1 %all-gather.15.cloned.1.call-start = ((), (), s32[]{:S(2)}) async-start(), calls=%async_computation.7 | async-start | bytes 1064960 | tf_op jit(solution)/shard_map/all_gather | solution.py:50
  19.2 328.6 %all-gather.9.cloned.1.call-start = ((), (), s32[]{:S(2)}) async-start(), calls=%async_computation.4 | async-start | bytes 1064960 | tf_op jit(solution)/shard_map/all_gather | solution.py:16
  101.8 21.7 %copy-start.6 = (f32[4,16]{1,0:T(4,128)S(1)}, f32[4,16]{1,0:T(4,128)}, u32[]{:S(2)}) copy-start(f32[4,16]{1,0:T(4,128)} %param.17) | copy-start | bytes 772
  101.8 23.6 %copy-start.5 = (bf16[32,1024]{1,0:T(8,128)(2,1)S(1)}, bf16[32,1024]{1,0:T(8,128)(2,1)}, u32[]{:S(2)}) copy-start(bf16[32,1024]{1,0:T(8,128)(2,1)} %param.19) | copy-start | bytes 196612
  123.8 0.6 copy-start.4
  124.4 305.9 %all-gather.11.cloned.1.call-start = ((), (), s32[]{:S(2)}) async-start(), calls=%async_computation.5 | async-start | bytes 1064960 | tf_op jit(solution)/shard_map/all_gather | solution.py:16
  124.8 0.6 copy-start.3
  126.1 354.1 %all-to-all-start.1 = ((bf16[32,8,128]{2,0,1:T(8,128)(2,1)}), bf16[32,8,128]{2,0,1:T(8,128)(2,1)}, u32[]{:S(2)}, u32[]{:S(2)}) async-start(bf16[32,8,128]{2,0,1:T(8,128)(2,1)} %copy_bitcast_fusion.2), calls=%async_computation.1 | async-start | bytes 131072 | tf_op jit(solution)/shard_map/all_to_all | solution.py:36
  264.6 4.1 copy-start.1
  268.7 211.7 %copy-start.2 = (bf16[256,128]{0,1:T(8,128)(2,1)S(1)}, bf16[256,128]{0,1:T(8,128)(2,1)}, u32[]{:S(2)}) copy-start(bf16[256,128]{0,1:T(8,128)(2,1)} %copy.174) | copy-start | bytes 196612
  835.3 9.6 %all-to-all-start.2 = ((bf16[8,32,128]{2,1,0:T(8,128)(2,1)}), bf16[8,32,128]{2,1,0:T(8,128)(2,1)S(1)}, u32[]{:S(2)}, u32[]{:S(2)}) async-start(bf16[8,32,128]{2,1,0:T(8,128)(2,1)} %bitcast.20), calls=%async_computation.2 | async-start | bytes 131072 | tf_op jit(solution)/shard_map/all_to_all | solution.py:148
  844.9 9.6 %all-to-all-start.3 = ((bf16[8,32,128]{2,1,0:T(8,128)(2,1)}), bf16[8,32,128]{2,1,0:T(8,128)(2,1)S(1)}, u32[]{:S(2)}, u32[]{:S(2)}) async-start(bf16[8,32,128]{2,1,0:T(8,128)(2,1)} %bitcast.22), calls=%async_computation.3 | async-start | bytes 131072 | tf_op jit(solution)/shard_map/all_to_all | solution.py:151
Sparse Core Ops, SparseCore 0:
  11.4 87.7 all-gather.12
  102.5 79.3 all-gather.16
  185.2 79.3 all-gather.14
  268.4 79.3 all-gather.8
  351.0 79.3 all-gather.10
where the time goes:
time: 875 us; the launch traced here: 862 us
  waiting for transfers between devices  378 us (43%)
  blocking collectives  303 us (35%)
  other arithmetic  53.9 us (6%)
  local copies, waits for them, and re-layouts  50.9 us (6%)
  starting transfers between devices  23.6 us (3%)
  matrix products  19.8 us (2%)
  loops' own time  17.9 us (2%)
  between operations  14.6 us (2%)
    unnamed x1, blocking collectives  303 us
    all_gather x2, waiting for transfers between devices, combined_all(): everything = jax.tree.map(lambda part: lax.all_gather(part, axis), x)  160 us
    all_gather x1, waiting for transfers between devices, shards(): lax.all_gather(grad_out, 'ctx', axis=0, tiled=True)  81 us
    all_gather x1, waiting for transfers between devices, shards(): lax.all_gather(queries, 'ctx', axis=0, tiled=True)  79.1 us
    all_gather x1, waiting for transfers between devices, shards(): lax.all_gather(outputs, 'ctx', axis=0, tiled=True)  48.3 us
    add x63, other arithmetic, combine_rows(): first_part[1] * jnp.exp(first_part[0] - higher)  47.9 us
  transfers between devices with their start and end apart: 9, of which 7 were waited for; matrix products, arithmetic and copies ran while one was open for 9% of the time, Pallas kernels for 0%

commit v1 on v0

v1 whole, which is shorter than its diff:
```python
import functools

import jax
import jax.numpy as jnp
from jax import lax
from jax.experimental import pallas as pl
from jax.experimental.pallas import tpu as pltpu
from jax.sharding import PartitionSpec as P

MESH = pl.DeviceIdType.MESH
F32 = jnp.float32
BF16 = jnp.bfloat16

DH = 128
HEADS = 8
PER_GROUP = 16
OWN_ROWS = 4
RESP_LEN = 64
YS, ZS = 4, 8
OWN_Q = OWN_ROWS * PER_GROUP
SLOTS = 2 * ZS
CHUNK = 2 * OWN_Q
NQ = SLOTS * OWN_Q
PIECE = 32
PIECES = 16
NT = 2 * PIECES * PIECE
SCALE = DH**-0.5
MASKED = -1e30
FLOOR = -1e20
DEAD = 1e30

NT_DIMS = (((1,), (1,)), ((), ()))


def kernel(
    q_in, do_in, o_in, lse_in, k_in, v_in, len_in, end_in,
    dq_out, dk_out, dv_out,
    qbuf, dobuf, kvs, kvbuf, lsebuf, mrow, lrow, posbuf, kt, ebuf, dsbuf, wq, wdo,
    dqs, dqr, fbuf, sib_s, sib_r, dkvs, dkvr,
    q_ss, q_rs, do_ss, do_rs, kv_ss, kv_rs, fwd_ss, fwd_rs, st_ss, st_rs, dq_ss, dq_rs,
    sib_ss, sib_rs, out_ss, out_rs,
):
    ctx = lax.axis_index("ctx")
    head = lax.axis_index("head")
    core = lax.rem(ctx, 2)
    z = lax.rem(ctx // 2, ZS)
    y = ctx // (2 * ZS)

    def device(yy, zz, cc, hh):
        return {
            "ctx": (lax.rem(yy + YS, YS) * ZS + lax.rem(zz + ZS, ZS)) * 2 + cc,
            "head": lax.rem(hh + HEADS, HEADS),
        }

    low = head < 4
    row_slots = [(s % 2 * 2, s // 2) for s in range(SLOTS)]

    def back_slot(dy, dz):
        return ((ZS - dz) % ZS) * 2 + dy // 2

    def row_device(s):
        dy, dz = row_slots[s]
        return device(y + dy, z + dz, core, head)

    def source_head(d):
        return lax.rem(head + HEADS - d, HEADS)

    def piece_y(p):
        if p < HEADS:
            return y
        return y + jnp.where(source_head(p - HEADS) < 4, 1, -1)

    def piece_device(p):
        return device(piece_y(p), z, core, source_head(p % HEADS))

    def user_device(p):
        if p < HEADS:
            return device(y, z, core, head + p)
        return device(y + jnp.where(low, -1, 1), z, core, head + p - HEADS)

    sibling = device(y, z, 1 - core, head)

    barrier = pltpu.get_barrier_semaphore()
    greeted = [row_device(s) for s in range(1, SLOTS)]
    greeted += [user_device(p) for p in range(1, PIECES)]
    greeted += [
        device(y + jnp.where(low, 1, -1), z, core, jnp.where(low, 0, 4) + i) for i in range(4)
    ]
    greeted += [sibling]
    for target in greeted:
        pl.semaphore_signal(barrier, inc=1, device_id=target, device_id_type=MESH)

    qbuf[0] = q_in[...]
    dobuf[0, :OWN_Q] = do_in[...]
    prod = do_in[...].astype(F32) * o_in[...].astype(F32)
    dots = jnp.sum(prod.T, axis=0, keepdims=True)
    dots = jnp.concatenate([dots, jnp.zeros((1, DH - OWN_Q), F32)], axis=1)
    high = dots.astype(BF16).astype(F32)
    middle = (dots - high).astype(BF16).astype(F32)
    rest = dots - high - middle
    dobuf[0, OWN_Q:] = jnp.concatenate(
        [high, middle, rest, jnp.zeros((13, DH), F32)], axis=0
    ).astype(BF16)
    for g in range(HEADS):
        kvs[g, 0] = k_in[:, g * DH : (g + 1) * DH]
        kvs[g, 1] = v_in[:, g * DH : (g + 1) * DH]
    pl.semaphore_wait(barrier, len(greeted))

    def copy(src, dst, ss, rs, i, target):
        return pltpu.make_async_remote_copy(
            src_ref=src, dst_ref=dst, send_sem=ss.at[i], recv_sem=rs.at[i],
            device_id=target, device_id_type=MESH,
        )

    sent = []

    def send(src, dst, ss, rs, i, target):
        started = copy(src, dst, ss, rs, i, target)
        started.start()
        sent.append(started)

    def kv_copy(p):
        return (
            kvs.at[lax.rem(head + p % HEADS, HEADS)], kvbuf.at[0, :, p], kv_ss, kv_rs, p,
            user_device(p),
        )

    for p in range(1, PIECES):
        send(*kv_copy(p))
    for s in range(1, SLOTS):
        t = back_slot(*row_slots[s])
        send(qbuf.at[0], qbuf.at[t], q_ss, q_rs, t, row_device(s))
    for s in range(1, SLOTS):
        t = back_slot(*row_slots[s])
        send(dobuf.at[0], dobuf.at[t], do_ss, do_rs, t, row_device(s))

    kvbuf[0, :, 0] = kvs[head]

    iota = lax.broadcasted_iota(jnp.int32, (PIECE, DH), 0)
    for part in range(2):
        part_core = core if part == 0 else 1 - core
        for p in range(PIECES):
            place = (lax.rem(piece_y(p) + YS, YS) * ZS + z) * 2 + part_core
            base = place * (HEADS * PIECE) + source_head(p % HEADS) * PIECE
            posbuf[pl.ds((part * PIECES + p) * PIECE, PIECE), :] = iota + base
    lane = lax.broadcasted_iota(jnp.int32, (1, DH), 1)
    limit = jnp.where(lane < OWN_Q, end_in[y], end_in[lax.rem(y + 2, YS)])

    lane64 = lax.broadcasted_iota(jnp.int32, (OWN_ROWS, OWN_Q), 1)
    sub64 = lax.broadcasted_iota(jnp.int32, (OWN_ROWS, OWN_Q), 0)
    spread = jnp.zeros((OWN_ROWS, OWN_Q), F32)
    for h in range(PER_GROUP):
        spread = jnp.where(lane64 // OWN_ROWS == h, lse_in[:, h : h + 1], spread)
    own_lse = jnp.sum(
        jnp.where(lane64 % OWN_ROWS == sub64, spread, 0.0), axis=0, keepdims=True
    )
    own_lse = jnp.concatenate([own_lse, jnp.full((1, DH - OWN_Q), MASKED, F32)], axis=1)
    row_in_resp = z * (2 * OWN_ROWS) + core * OWN_ROWS + lane % OWN_ROWS
    dead = jnp.logical_and(lane < OWN_Q, row_in_resp >= len_in[y])

    for p in range(1, PIECES):
        copy(*kv_copy(p)).wait_recv()
    for i in range(2):
        send(kvbuf.at[0, i], kvbuf.at[1, i], fwd_ss, fwd_rs, i, sibling)
    for i in range(2):
        copy(kvbuf.at[0, i], kvbuf.at[1, i], fwd_ss, fwd_rs, i, sibling).wait_recv()
    for s in range(1, SLOTS):
        copy(qbuf.at[0], qbuf.at[s], q_ss, q_rs, s, sibling).wait_recv()

    keys = kvbuf[:, 0].reshape(NT, DH)
    kt[...] = keys.T

    def score_step(c, carry):
        queries = qbuf[pl.ds(2 * c, 2)].reshape(CHUNK, DH)
        scores = lax.dot_general(
            kvbuf[:, 0].reshape(NT, DH), queries, NT_DIMS, preferred_element_type=F32
        ) * SCALE
        scores = jnp.where(posbuf[...] < limit, scores, MASKED)
        peak = jnp.maximum(jnp.max(scores, axis=0, keepdims=True), FLOOR)
        terms = jnp.exp(scores - peak)
        total = jnp.sum(terms, axis=0, keepdims=True)
        ebuf[:, pl.ds(pl.multiple_of(c * CHUNK, CHUNK), CHUNK)] = terms.astype(BF16)
        mrow[pl.ds(c, 1), :] = peak
        lrow[pl.ds(c, 1), :] = total
        return carry

    lax.fori_loop(0, SLOTS // 2, score_step, 0)

    peaks = mrow[...]
    totals = lrow[...]
    local_lse = jnp.where(totals > 0.0, peaks + jnp.log(jnp.maximum(totals, 1e-37)), MASKED)
    first = local_lse[0:1]
    higher = jnp.maximum(first, own_lse)
    joined = higher + jnp.log(jnp.exp(first - higher) + jnp.exp(own_lse - higher))
    joined = jnp.where(lane < OWN_Q, jnp.where(dead, DEAD, joined), first)
    lsebuf[0] = jnp.concatenate([joined, local_lse[1:]], axis=0)
    for s in range(1, SLOTS):
        t = back_slot(*row_slots[s])
        send(lsebuf.at[0], lsebuf.at[t], st_ss, st_rs, t, row_device(s))
    lrow[...] = jnp.where(totals > 0.0, SCALE / jnp.maximum(totals, 1e-37), 0.0)

    for s in range(1, SLOTS):
        copy(dobuf.at[0], dobuf.at[s], do_ss, do_rs, s, sibling).wait_recv()

    def dscore_step(c, carry):
        pair = dobuf[pl.ds(2 * c, 2)]
        grads = pair[:, :OWN_Q].reshape(CHUNK, DH)
        parts = pair[:, OWN_Q:].astype(F32)
        dots_pair = parts[:, 0:1] + parts[:, 1:2] + parts[:, 2:3]
        dots_row = jnp.concatenate([dots_pair[0, :, :OWN_Q], dots_pair[1, :, :OWN_Q]], axis=1)
        dprob = lax.dot_general(
            kvbuf[:, 1].reshape(NT, DH), grads, NT_DIMS, preferred_element_type=F32
        )
        columns = pl.ds(pl.multiple_of(c * CHUNK, CHUNK), CHUNK)
        dscore = (ebuf[:, columns].astype(F32) * (dprob - dots_row)).astype(BF16)
        dsbuf[:, columns] = dscore
        dq_t = jnp.dot(kt[...], dscore, preferred_element_type=F32)
        dq_t = dq_t * lrow[pl.ds(c, 1), :]
        dqs[pl.ds(2 * c, 2)] = dq_t.T.astype(BF16).reshape(2, OWN_Q, DH)
        return carry

    lax.fori_loop(0, SLOTS // 2, dscore_step, 0)

    for s in range(1, SLOTS):
        t = back_slot(*row_slots[s])
        send(dqs.at[s], dqr.at[t], dq_ss, dq_rs, t, row_device(s))

    aligned = []
    for s in range(SLOTS):
        if s > 0:
            copy(lsebuf.at[0], lsebuf.at[s], st_ss, st_rs, s, sibling).wait_recv()
        part = lsebuf[s]
        dy, dz = row_slots[s]
        if dz:
            part = jnp.concatenate([part[ZS - dz :], part[: ZS - dz]], axis=0)
        if dy:
            part = jnp.concatenate([part[:, OWN_Q:], part[:, :OWN_Q]], axis=1)
        aligned.append(part)
    top = functools.reduce(jnp.maximum, aligned)
    total = functools.reduce(jnp.add, [jnp.exp(part - top) for part in aligned])
    full_lse = top + jnp.log(total)
    for s in range(SLOTS):
        mine = local_lse[0:1] if s == 0 else aligned[s][0:1]
        fbuf[s : s + 1, :] = jnp.exp(mine - full_lse[0:1])
    weight = jnp.exp(peaks - full_lse).T
    for c in range(SLOTS // 2):
        rows = slice(c * CHUNK, (c + 1) * CHUNK)
        column = weight[:, c : c + 1]
        wq[rows] = (
            qbuf[2 * c : 2 * c + 2].reshape(CHUNK, DH).astype(F32) * (column * SCALE)
        ).astype(BF16)
        wdo[rows] = (
            dobuf[2 * c : 2 * c + 2, :OWN_Q].reshape(CHUNK, DH).astype(F32) * column
        ).astype(BF16)

    half = PIECES * PIECE
    block = 256
    for i, (probs, weighted) in enumerate(((dsbuf, wq), (ebuf, wdo))):
        for b in range(half // block):
            rows = slice(half + b * block, half + (b + 1) * block)
            part = jnp.dot(probs[rows], weighted[...], preferred_element_type=F32)
            per = block // PIECE
            sib_s[i, b * per : (b + 1) * per] = part.astype(BF16).reshape(per, PIECE, DH)
        send(sib_s.at[i], sib_r.at[i], sib_ss, sib_rs, i, sibling)
    for i, (probs, weighted) in enumerate(((dsbuf, wq), (ebuf, wdo))):
        copy(sib_s.at[i], sib_r.at[i], sib_ss, sib_rs, i, sibling).wait_recv()
        for b in range(half // block):
            rows = slice(b * block, (b + 1) * block)
            part = jnp.dot(probs[rows], weighted[...], preferred_element_type=F32)
            per = block // PIECE
            pieces = slice(b * per, (b + 1) * per)
            dkvs[i, pieces] = (
                part.reshape(per, PIECE, DH) + sib_r[i, pieces].astype(F32)
            ).astype(BF16)

    for p in range(1, PIECES):
        send(dkvs.at[:, p], dkvr.at[p], out_ss, out_rs, p, piece_device(p))
    dkvr[0] = dkvs[:, 0]

    shares = fbuf[...].T
    grad = dqs[0].astype(F32) * shares[:OWN_Q, 0:1]
    for s in range(1, SLOTS):
        copy(dqs.at[0], dqr.at[s], dq_ss, dq_rs, s, sibling).wait_recv()
        grad = grad + dqr[s].astype(F32) * shares[:OWN_Q, s : s + 1]
    dq_out[...] = grad.astype(BF16)

    for p in range(1, PIECES):
        copy(dkvs.at[:, 0], dkvr.at[p], out_ss, out_rs, p, sibling).wait_recv()
    for d in range(HEADS):
        total = dkvr[d].astype(F32) + dkvr[HEADS + d].astype(F32)
        columns = pl.ds(pl.multiple_of(lax.rem(head + d, HEADS) * DH, DH), DH)
        dk_out[:, columns] = total[0].astype(BF16)
        dv_out[:, columns] = total[1].astype(BF16)

    for started in sent:
        started.wait_send()


def to_vectors(x):
    return x.reshape(OWN_ROWS, PER_GROUP, DH).transpose(1, 0, 2).reshape(OWN_Q, DH)


def shards(queries, grad_out, outputs, lse_self, prompt_keys, prompt_values, resp_len, prompt_end):
    vmem = pl.BlockSpec(memory_space=pltpu.VMEM)
    smem = pl.BlockSpec(memory_space=pltpu.SMEM)

    def dma(n):
        return [pltpu.SemaphoreType.DMA((n,)), pltpu.SemaphoreType.DMA((n,))]

    dq, dk, dv = pl.pallas_call(
        kernel,
        out_shape=(
            jax.ShapeDtypeStruct((OWN_Q, DH), BF16),
            jax.ShapeDtypeStruct((PIECE, HEADS * DH), BF16),
            jax.ShapeDtypeStruct((PIECE, HEADS * DH), BF16),
        ),
        in_specs=[vmem] * 6 + [smem] * 2,
        out_specs=(vmem, vmem, vmem),
        scratch_shapes=[
            pltpu.VMEM((SLOTS, OWN_Q, DH), BF16),
            pltpu.VMEM((SLOTS, OWN_Q + 16, DH), BF16),
            pltpu.VMEM((HEADS, 2, PIECE, DH), BF16),
            pltpu.VMEM((2, 2, PIECES, PIECE, DH), BF16),
            pltpu.VMEM((SLOTS, ZS, DH), F32),
            pltpu.VMEM((ZS, DH), F32),
            pltpu.VMEM((ZS, DH), F32),
            pltpu.VMEM((NT, DH), jnp.int32),
            pltpu.VMEM((DH, NT), BF16),
            pltpu.VMEM((NT, NQ), BF16),
            pltpu.VMEM((NT, NQ), BF16),
            pltpu.VMEM((NQ, DH), BF16),
            pltpu.VMEM((NQ, DH), BF16),
            pltpu.VMEM((SLOTS, OWN_Q, DH), BF16),
            pltpu.VMEM((SLOTS, OWN_Q, DH), BF16),
            pltpu.VMEM((SLOTS, DH), F32),
            pltpu.VMEM((2, PIECES, PIECE, DH), BF16),
            pltpu.VMEM((2, PIECES, PIECE, DH), BF16),
            pltpu.VMEM((2, PIECES, PIECE, DH), BF16),
            pltpu.VMEM((PIECES, 2, PIECE, DH), BF16),
        ]
        + dma(SLOTS) + dma(SLOTS) + dma(PIECES) + dma(2) + dma(SLOTS) + dma(SLOTS)
        + dma(2) + dma(PIECES),
        compiler_params=pltpu.CompilerParams(
            collective_id=0, has_side_effects=True, vmem_limit_bytes=40 << 20
        ),
    )(
        to_vectors(queries), to_vectors(grad_out), to_vectors(outputs), lse_self,
        prompt_keys, prompt_values, resp_len, prompt_end,
    )
    query_grad = (
        dq.reshape(PER_GROUP, OWN_ROWS, DH).transpose(1, 0, 2).reshape(OWN_ROWS, PER_GROUP * DH)
    )
    return query_grad, dk, dv


def solution(mesh):
    in_specs = (
        P("ctx", "head"),
        P("ctx", "head"),
        P("ctx", "head"),
        P("ctx", "head"),
        P(("ctx", "head"), None),
        P(("ctx", "head"), None),
        P(),
        P(),
    )
    out_specs = (P("ctx", "head"), P(("ctx", "head"), None), P(("ctx", "head"), None))
    return jax.shard_map(shards, mesh=mesh, in_specs=in_specs, out_specs=out_specs, check_vma=False)
```

time: 875 us -> 65.1 us (0.07)
  the two profiles are of different devices: /device:TPU:2 before, /device:TPU:1 now
where the time goes in v1:
time: 65.1 us; the launch traced here: 63.9 us
  Pallas kernels  56.9 us (87%)
  local copies, waits for them, and re-layouts  6.36 us (10%)
  between operations  0.67 us (1%)
    pallas_call x1, Pallas kernels, shards(): pl.pallas_call(kernel, out_shape=(jax.ShapeDtypeStruct((OWN_Q, DH), BF16)...  56.9 us
    unnamed x19, local copies, waits for them, and re-layouts  6.36 us

profile of v1, /device:TPU:1, one launch (start us, length us, event | category | flops | bytes accessed | tf_op | source)
XLA Modules:
  0.0 63.9 jit_solution(23085888315952087)
XLA Ops:
  0.6 0.0 copy-start.5
  0.6 0.0 copy-start.6
  0.7 0.0 copy-start.7
  0.7 0.7 %copy-done.5 = f32[4,16]{1,0:T(4,128)S(1)} copy-done((f32[4,16]{1,0:T(4,128)S(1)}, f32[4,16]{1,0:T(4,128)}, u32[]{:S(2)}) %copy-start.5) | copy-done | bytes 280
  1.3 0.0 copy-done.6
  1.3 0.0 copy-done.7
  1.3 0.0 copy-start
  1.3 0.8 %copy-done = bf16[32,1024]{1,0:T(8,128)(2,1)S(1)} copy-done((bf16[32,1024]{1,0:T(8,128)(2,1)S(1)}, bf16[32,1024]{1,0:T(8,128)(2,1)}, u32[]{:S(2)}) %copy-start) | copy-done | bytes 65560
  2.2 0.0 copy-start.1
  2.2 0.8 %copy-done.1 = bf16[32,1024]{1,0:T(8,128)(2,1)S(1)} copy-done((bf16[32,1024]{1,0:T(8,128)(2,1)S(1)}, bf16[32,1024]{1,0:T(8,128)(2,1)}, u32[]{:S(2)}) %copy-start.1) | copy-done | bytes 65560
  3.0 0.0 copy-start.2
  3.0 0.7 %copy-done.2 = bf16[4,2048]{1,0:T(4,128)(2,1)S(1)} copy-done((bf16[4,2048]{1,0:T(4,128)(2,1)S(1)}, bf16[4,2048]{1,0:T(4,128)(2,1)}, u32[]{:S(2)}) %copy-start.2) | copy-done | bytes 16408
  3.7 0.0 copy-start.3
  3.7 0.7 %copy-done.3 = bf16[4,2048]{1,0:T(4,128)(2,1)S(1)} copy-done((bf16[4,2048]{1,0:T(4,128)(2,1)S(1)}, bf16[4,2048]{1,0:T(4,128)(2,1)}, u32[]{:S(2)}) %copy-start.3) | copy-done | bytes 16408
  4.4 0.0 copy-start.4
  4.4 0.7 %copy-done.4 = bf16[4,2048]{1,0:T(4,128)(2,1)S(1)} copy-done((bf16[4,2048]{1,0:T(4,128)(2,1)S(1)}, bf16[4,2048]{1,0:T(4,128)(2,1)}, u32[]{:S(2)}) %copy-start.4) | copy-done | bytes 16408
  5.2 56.9 %shard_map.103 = (bf16[64,128]{1,0:T(8,128)(2,1)S(1)}, bf16[32,1024]{1,0:T(8,128)(2,1)S(1)}, bf16[32,1024]{1,0:T(8,128)(2,1)S(1)}) custom-call(bf16[64,128]{1,0:T(8,128)(2,1)S(1)} %bitcast.20, bf16[64,128]{1,0:T(8,128)(2,1)S(1)} %bitcast.21, bf16[64,128]{1,0:T(8,128)(2,1)S(1)} %bitcast.22, f32[4,16]{1,0:T(4,128)S(1)} %copy-done.5, ...), custom_call_target="tpu_custom_call" | custom-call | tf_op jit(solution)/shard_map/pallas_call | solution.py:310
  62.1 0.6 copy.18
  62.7 0.6 copy.19
  63.3 0.6 copy.20
Async XLA Ops:
  0.6 0.7 %copy-start.5 = (f32[4,16]{1,0:T(4,128)S(1)}, f32[4,16]{1,0:T(4,128)}, u32[]{:S(2)}) copy-start(f32[4,16]{1,0:T(4,128)} %lse_in.1) | copy-start | bytes 772
  0.6 0.7 %copy-start.6 = (s32[4]{0:T(128)S(1)}, s32[4]{0:T(128)}, u32[]{:S(2)}) copy-start(s32[4]{0:T(128)} %len_in.1) | copy-start | bytes 52
  0.7 0.7 %copy-start.7 = (s32[4]{0:T(128)S(1)}, s32[4]{0:T(128)}, u32[]{:S(2)}) copy-start(s32[4]{0:T(128)} %end_in.1) | copy-start | bytes 52
  1.3 0.8 %copy-start = (bf16[32,1024]{1,0:T(8,128)(2,1)S(1)}, bf16[32,1024]{1,0:T(8,128)(2,1)}, u32[]{:S(2)}) copy-start(bf16[32,1024]{1,0:T(8,128)(2,1)} %k_in.1) | copy-start | bytes 196612
  2.2 0.8 %copy-start.1 = (bf16[32,1024]{1,0:T(8,128)(2,1)S(1)}, bf16[32,1024]{1,0:T(8,128)(2,1)}, u32[]{:S(2)}) copy-start(bf16[32,1024]{1,0:T(8,128)(2,1)} %v_in.1) | copy-start | bytes 196612
  3.0 0.7 %copy-start.2 = (bf16[4,2048]{1,0:T(4,128)(2,1)S(1)}, bf16[4,2048]{1,0:T(4,128)(2,1)}, u32[]{:S(2)}) copy-start(bf16[4,2048]{1,0:T(4,128)(2,1)} %param.8) | copy-start | bytes 49156
  3.7 0.7 %copy-start.3 = (bf16[4,2048]{1,0:T(4,128)(2,1)S(1)}, bf16[4,2048]{1,0:T(4,128)(2,1)}, u32[]{:S(2)}) copy-start(bf16[4,2048]{1,0:T(4,128)(2,1)} %param.9) | copy-start | bytes 49156
  4.4 0.7 %copy-start.4 = (bf16[4,2048]{1,0:T(4,128)(2,1)S(1)}, bf16[4,2048]{1,0:T(4,128)(2,1)}, u32[]{:S(2)}) copy-start(bf16[4,2048]{1,0:T(4,128)(2,1)} %param.10) | copy-start | bytes 49156

commit v2 on v1

--- a/solution.py
+++ b/solution.py
@@ -32,12 +32,44 @@
 NT_DIMS = (((1,), (1,)), ((), ()))
 
 
+def realigned(part, dy, dz):
+    halves = []
+    for group in range(2):
+        rows = part[group * 4 : group * 4 + 4]
+        left, right = rows[:, :OWN_Q], rows[:, OWN_Q:]
+        if dz % 2:
+            left, right = rolled(right, dz // 2 + 1), rolled(left, dz // 2)
+        else:
+            left, right = rolled(left, dz // 2), rolled(right, dz // 2)
+        halves.append(jnp.concatenate([left, right], axis=1))
+    if dy:
+        halves.reverse()
+    return jnp.concatenate(halves, axis=0)
+
+
+def rolled(x, by):
+    by = by % 4
+    return jnp.concatenate([x[4 - by :], x[: 4 - by]], axis=0) if by else x
+
+
+def write_out(dq_in, dk_in, dv_in, dq_out, dk_out, dv_out, sems):
+    copies = [
+        pltpu.make_async_copy(src, dst, sems.at[i])
+        for i, (src, dst) in enumerate(((dk_in, dk_out), (dv_in, dv_out), (dq_in, dq_out)))
+    ]
+    for copy in copies:
+        copy.start()
+    for copy in copies:
+        copy.wait()
+
+
 def kernel(
-    q_in, do_in, o_in, lse_in, k_in, v_in, len_in, end_in,
+    q_hbm, do_hbm, o_hbm, lse_hbm, k_hbm, v_hbm, len_hbm, end_hbm,
     dq_out, dk_out, dv_out,
+    o_in, lse_in, k_in, v_in, len_in, end_in, in_sems,
     qbuf, dobuf, kvs, kvbuf, lsebuf, mrow, lrow, posbuf, kt, ebuf, dsbuf, wq, wdo,
-    dqs, dqr, fbuf, sib_s, sib_r, dkvs, dkvr,
-    q_ss, q_rs, do_ss, do_rs, kv_ss, kv_rs, fwd_ss, fwd_rs, st_ss, st_rs, dq_ss, dq_rs,
+    dqs, dqr, dqy_s, dqy_r, fbuf, sib_s, sib_r, dkvs, dkvr,
+    q_ss, q_rs, do_ss, do_rs, kv_ss, kv_rs, fwd_ss, fwd_rs, st_ss, st_rs, dq_ss, dq_rs, dqy_ss, dqy_rs,
     sib_ss, sib_rs, out_ss, out_rs,
 ):
     ctx = lax.axis_index("ctx")
@@ -53,10 +85,10 @@
         }
 
     low = head < 4
-    row_slots = [(s % 2 * 2, s // 2) for s in range(SLOTS)]
+    row_slots = [(s // ZS * 2, s % ZS) for s in range(SLOTS)]
 
     def back_slot(dy, dz):
-        return ((ZS - dz) % ZS) * 2 + dy // 2
+        return dy // 2 * ZS + (ZS - dz) % ZS
 
     def row_device(s):
         dy, dz = row_slots[s]
@@ -79,9 +111,21 @@
         return device(y + jnp.where(low, -1, 1), z, core, head + p - HEADS)
 
     sibling = device(y, z, 1 - core, head)
+    across = row_device(ZS)
+
+    arrivals = [
+        pltpu.make_async_copy(src, dst, in_sems.at[i])
+        for i, (src, dst) in enumerate((
+            (q_hbm, qbuf.at[0]), (do_hbm, dobuf.at[0, pl.ds(0, OWN_Q)]), (k_hbm, k_in),
+            (v_hbm, v_in), (o_hbm, o_in), (lse_hbm, lse_in), (len_hbm, len_in),
+            (end_hbm, end_in),
+        ))
+    ]
+    for arrival in arrivals:
+        arrival.start()
 
     barrier = pltpu.get_barrier_semaphore()
-    greeted = [row_device(s) for s in range(1, SLOTS)]
+    greeted = [row_device(s) for s in range(1, ZS + 1)]
     greeted += [user_device(p) for p in range(1, PIECES)]
     greeted += [
         device(y + jnp.where(low, 1, -1), z, core, jnp.where(low, 0, 4) + i) for i in range(4)
@@ -90,9 +134,9 @@
     for target in greeted:
         pl.semaphore_signal(barrier, inc=1, device_id=target, device_id_type=MESH)
 
-    qbuf[0] = q_in[...]
-    dobuf[0, :OWN_Q] = do_in[...]
-    prod = do_in[...].astype(F32) * o_in[...].astype(F32)
+    for arrival in arrivals:
+        arrival.wait()
+    prod = dobuf[0, :OWN_Q].astype(F32) * o_in[...].astype(F32)
     dots = jnp.sum(prod.T, axis=0, keepdims=True)
     dots = jnp.concatenate([dots, jnp.zeros((1, DH - OWN_Q), F32)], axis=1)
     high = dots.astype(BF16).astype(F32)
@@ -125,14 +169,16 @@
             user_device(p),
         )
 
+    def send_along(buf, ss, rs, s):
+        for dz in range(1, ZS):
+            send(buf.at[s], buf.at[s + ZS - dz], ss, rs, s + ZS - dz, row_device(dz))
+
+    send(qbuf.at[0], qbuf.at[ZS], q_ss, q_rs, ZS, across)
+    send(dobuf.at[0], dobuf.at[ZS], do_ss, do_rs, ZS, across)
     for p in range(1, PIECES):
         send(*kv_copy(p))
-    for s in range(1, SLOTS):
-        t = back_slot(*row_slots[s])
-        send(qbuf.at[0], qbuf.at[t], q_ss, q_rs, t, row_device(s))
-    for s in range(1, SLOTS):
-        t = back_slot(*row_slots[s])
-        send(dobuf.at[0], dobuf.at[t], do_ss, do_rs, t, row_device(s))
+    send_along(qbuf, q_ss, q_rs, 0)
+    send_along(dobuf, do_ss, do_rs, 0)
 
     kvbuf[0, :, 0] = kvs[head]
 
@@ -144,7 +190,7 @@
             base = place * (HEADS * PIECE) + source_head(p % HEADS) * PIECE
             posbuf[pl.ds((part * PIECES + p) * PIECE, PIECE), :] = iota + base
     lane = lax.broadcasted_iota(jnp.int32, (1, DH), 1)
-    limit = jnp.where(lane < OWN_Q, end_in[y], end_in[lax.rem(y + 2, YS)])
+    limits = (end_in[y], end_in[lax.rem(y + 2, YS)])
 
     lane64 = lax.broadcasted_iota(jnp.int32, (OWN_ROWS, OWN_Q), 1)
     sub64 = lax.broadcasted_iota(jnp.int32, (OWN_ROWS, OWN_Q), 0)
@@ -158,19 +204,30 @@
     row_in_resp = z * (2 * OWN_ROWS) + core * OWN_ROWS + lane % OWN_ROWS
     dead = jnp.logical_and(lane < OWN_Q, row_in_resp >= len_in[y])
 
+    copy(qbuf.at[0], qbuf.at[ZS], q_ss, q_rs, ZS, sibling).wait_recv()
+    send_along(qbuf, q_ss, q_rs, ZS)
+    copy(dobuf.at[0], dobuf.at[ZS], do_ss, do_rs, ZS, sibling).wait_recv()
+    send_along(dobuf, do_ss, do_rs, ZS)
+
     for p in range(1, PIECES):
         copy(*kv_copy(p)).wait_recv()
     for i in range(2):
         send(kvbuf.at[0, i], kvbuf.at[1, i], fwd_ss, fwd_rs, i, sibling)
     for i in range(2):
         copy(kvbuf.at[0, i], kvbuf.at[1, i], fwd_ss, fwd_rs, i, sibling).wait_recv()
-    for s in range(1, SLOTS):
-        copy(qbuf.at[0], qbuf.at[s], q_ss, q_rs, s, sibling).wait_recv()
-
     keys = kvbuf[:, 0].reshape(NT, DH)
     kt[...] = keys.T
 
+    def wait_pair(buf, ss, rs, c):
+        @pl.when(lax.rem(c, ZS // 2) > 0)
+        def _():
+            copy(buf.at[0], buf.at[2 * c], ss, rs, 2 * c, sibling).wait_recv()
+
+        copy(buf.at[0], buf.at[2 * c + 1], ss, rs, 2 * c + 1, sibling).wait_recv()
+
     def score_step(c, carry):
+        wait_pair(qbuf, q_ss, q_rs, c)
+        limit = jnp.where(c < ZS // 2, limits[0], limits[1])
         queries = qbuf[pl.ds(2 * c, 2)].reshape(CHUNK, DH)
         scores = lax.dot_general(
             kvbuf[:, 0].reshape(NT, DH), queries, NT_DIMS, preferred_element_type=F32
@@ -199,10 +256,8 @@
         send(lsebuf.at[0], lsebuf.at[t], st_ss, st_rs, t, row_device(s))
     lrow[...] = jnp.where(totals > 0.0, SCALE / jnp.maximum(totals, 1e-37), 0.0)
 
-    for s in range(1, SLOTS):
-        copy(dobuf.at[0], dobuf.at[s], do_ss, do_rs, s, sibling).wait_recv()
-
     def dscore_step(c, carry):
+        wait_pair(dobuf, do_ss, do_rs, c)
         pair = dobuf[pl.ds(2 * c, 2)]
         grads = pair[:, :OWN_Q].reshape(CHUNK, DH)
         parts = pair[:, OWN_Q:].astype(F32)
@@ -221,9 +276,10 @@
 
     lax.fori_loop(0, SLOTS // 2, dscore_step, 0)
 
-    for s in range(1, SLOTS):
-        t = back_slot(*row_slots[s])
-        send(dqs.at[s], dqr.at[t], dq_ss, dq_rs, t, row_device(s))
+    for s in (0, ZS):
+        for dz in range(1, ZS):
+            t = s + ZS - dz
+            send(dqs.at[s + dz], dqr.at[t], dq_ss, dq_rs, t, row_device(dz))
 
     aligned = []
     for s in range(SLOTS):
@@ -231,17 +287,14 @@
             copy(lsebuf.at[0], lsebuf.at[s], st_ss, st_rs, s, sibling).wait_recv()
         part = lsebuf[s]
         dy, dz = row_slots[s]
-        if dz:
-            part = jnp.concatenate([part[ZS - dz :], part[: ZS - dz]], axis=0)
-        if dy:
-            part = jnp.concatenate([part[:, OWN_Q:], part[:, :OWN_Q]], axis=1)
-        aligned.append(part)
+        aligned.append(realigned(part, dy, dz))
     top = functools.reduce(jnp.maximum, aligned)
     total = functools.reduce(jnp.add, [jnp.exp(part - top) for part in aligned])
     full_lse = top + jnp.log(total)
-    for s in range(SLOTS):
-        mine = local_lse[0:1] if s == 0 else aligned[s][0:1]
-        fbuf[s : s + 1, :] = jnp.exp(mine - full_lse[0:1])
+    for dz in range(ZS):
+        for s, row in ((0, 0), (ZS, ZS // 2)):
+            mine = local_lse[row : row + 1] if dz == 0 else aligned[dz][row : row + 1]
+            fbuf[s + dz : s + dz + 1, :] = jnp.exp(mine - full_lse[row : row + 1])
     weight = jnp.exp(peaks - full_lse).T
     for c in range(SLOTS // 2):
         rows = slice(c * CHUNK, (c + 1) * CHUNK)
@@ -278,11 +331,19 @@
     dkvr[0] = dkvs[:, 0]
 
     shares = fbuf[...].T
-    grad = dqs[0].astype(F32) * shares[:OWN_Q, 0:1]
-    for s in range(1, SLOTS):
-        copy(dqs.at[0], dqr.at[s], dq_ss, dq_rs, s, sibling).wait_recv()
-        grad = grad + dqr[s].astype(F32) * shares[:OWN_Q, s : s + 1]
-    dq_out[...] = grad.astype(BF16)
+
+    def summed(s):
+        grad = dqs[s].astype(F32) * shares[:OWN_Q, s : s + 1]
+        for t in range(s + 1, s + ZS):
+            copy(dqs.at[0], dqr.at[t], dq_ss, dq_rs, t, sibling).wait_recv()
+            grad = grad + dqr[t].astype(F32) * shares[:OWN_Q, t : t + 1]
+        return grad
+
+    dqy_s[...] = summed(ZS)
+    send(dqy_s, dqy_r, dqy_ss, dqy_rs, 0, across)
+    grad = summed(0)
+    copy(dqy_s, dqy_r, dqy_ss, dqy_rs, 0, sibling).wait_recv()
+    dq_out[...] = (grad + dqy_r[...]).astype(BF16)
 
     for p in range(1, PIECES):
         copy(dkvs.at[:, 0], dkvr.at[p], out_ss, out_rs, p, sibling).wait_recv()
@@ -302,21 +363,29 @@
 
 def shards(queries, grad_out, outputs, lse_self, prompt_keys, prompt_values, resp_len, prompt_end):
     vmem = pl.BlockSpec(memory_space=pltpu.VMEM)
-    smem = pl.BlockSpec(memory_space=pltpu.SMEM)
+    anywhere = pl.BlockSpec(memory_space=pltpu.HBM)
 
     def dma(n):
         return [pltpu.SemaphoreType.DMA((n,)), pltpu.SemaphoreType.DMA((n,))]
 
-    dq, dk, dv = pl.pallas_call(
+    out_shape = (
+        jax.ShapeDtypeStruct((OWN_Q, DH), BF16),
+        jax.ShapeDtypeStruct((PIECE, HEADS * DH), BF16),
+        jax.ShapeDtypeStruct((PIECE, HEADS * DH), BF16),
+    )
+    grads = pl.pallas_call(
         kernel,
-        out_shape=(
-            jax.ShapeDtypeStruct((OWN_Q, DH), BF16),
-            jax.ShapeDtypeStruct((PIECE, HEADS * DH), BF16),
-            jax.ShapeDtypeStruct((PIECE, HEADS * DH), BF16),
-        ),
-        in_specs=[vmem] * 6 + [smem] * 2,
+        out_shape=out_shape,
+        in_specs=[anywhere] * 8,
         out_specs=(vmem, vmem, vmem),
         scratch_shapes=[
+            pltpu.VMEM((OWN_Q, DH), BF16),
+            pltpu.VMEM((OWN_ROWS, PER_GROUP), F32),
+            pltpu.VMEM((PIECE, HEADS * DH), BF16),
+            pltpu.VMEM((PIECE, HEADS * DH), BF16),
+            pltpu.SMEM((YS,), jnp.int32),
+            pltpu.SMEM((YS,), jnp.int32),
+            pltpu.SemaphoreType.DMA((8,)),
             pltpu.VMEM((SLOTS, OWN_Q, DH), BF16),
             pltpu.VMEM((SLOTS, OWN_Q + 16, DH), BF16),
             pltpu.VMEM((HEADS, 2, PIECE, DH), BF16),
@@ -332,6 +401,8 @@
             pltpu.VMEM((NQ, DH), BF16),
             pltpu.VMEM((SLOTS, OWN_Q, DH), BF16),
             pltpu.VMEM((SLOTS, OWN_Q, DH), BF16),
+            pltpu.VMEM((OWN_Q, DH), F32),
+            pltpu.VMEM((OWN_Q, DH), F32),
             pltpu.VMEM((SLOTS, DH), F32),
             pltpu.VMEM((2, PIECES, PIECE, DH), BF16),
             pltpu.VMEM((2, PIECES, PIECE, DH), BF16),
@@ -339,14 +410,22 @@
             pltpu.VMEM((PIECES, 2, PIECE, DH), BF16),
         ]
         + dma(SLOTS) + dma(SLOTS) + dma(PIECES) + dma(2) + dma(SLOTS) + dma(SLOTS)
-        + dma(2) + dma(PIECES),
+        + dma(1) + dma(2) + dma(PIECES),
         compiler_params=pltpu.CompilerParams(
-            collective_id=0, has_side_effects=True, vmem_limit_bytes=40 << 20
+            collective_id=0, has_side_effects=True, vmem_limit_bytes=64 << 20
         ),
     )(
         to_vectors(queries), to_vectors(grad_out), to_vectors(outputs), lse_self,
         prompt_keys, prompt_values, resp_len, prompt_end,
     )
+    dq, dk, dv = pl.pallas_call(
+        write_out,
+        out_shape=out_shape,
+        in_specs=[vmem] * 3,
+        out_specs=(anywhere, anywhere, anywhere),
+        scratch_shapes=[pltpu.SemaphoreType.DMA((3,))],
+        compiler_params=pltpu.CompilerParams(vmem_limit_bytes=64 << 20),
+    )(*grads)
     query_grad = (
         dq.reshape(PER_GROUP, OWN_ROWS, DH).transpose(1, 0, 2).reshape(OWN_ROWS, PER_GROUP * DH)
     )

time: 65.1 us -> 52.2 us (0.80); the launches traced: 63.9 us -> 52 us
  local copies, waits for them, and re-layouts: 6.36 us -> 0 us
  Pallas kernels: 56.9 us -> 51.3 us
    unnamed x19 -> x0, local copies, waits for them, and re-layouts: 6.36 us -> none
    pallas_call x1 -> x2, Pallas kernels: 56.9 us -> 51.3 us  [the longest x1 49.7 us: shards(): pl.pallas_call(kernel, out_shape=out_shape, in_specs=[anywhere] * 8, out_...]
where the time goes in v2:
time: 52.2 us; the launch traced here: 52 us
  Pallas kernels  51.3 us (98%)
  between operations  0.64 us (1%)
    pallas_call x1, Pallas kernels, shards(): pl.pallas_call(kernel, out_shape=out_shape, in_specs=[anywhere] * 8, out_...  49.7 us
    pallas_call x1, Pallas kernels, shards(): pl.pallas_call(write_out, out_shape=out_shape, in_specs=[vmem] * 3, out_s...  1.57 us

profile of v2, /device:TPU:1, one launch (start us, length us, event | category | flops | bytes accessed | tf_op | source)
XLA Modules:
  0.0 52.0 jit_solution(1748750300153960949)
XLA Ops:
  0.6 49.7 %shard_map.103 = (bf16[64,128]{1,0:T(8,128)(2,1)}, bf16[32,1024]{1,0:T(8,128)(2,1)}, bf16[32,1024]{1,0:T(8,128)(2,1)}) custom-call(bf16[64,128]{1,0:T(8,128)(2,1)} %bitcast.20, bf16[64,128]{1,0:T(8,128)(2,1)} %bitcast.21, bf16[64,128]{1,0:T(8,128)(2,1)} %bitcast.22, f32[4,16]{1,0:T(4,128)} %lse_hbm.1, bf16[32,1024]{1,0:T(8,128)(2,1)} %k_hbm.1, ...), custom_call_target="tpu_custom_call" | custom-call | tf_op jit(solution)/shard_map/pallas_call | solution.py:376
  50.4 1.6 %shard_map.104 = (bf16[64,128]{1,0:T(8,128)(2,1)}, bf16[32,1024]{1,0:T(8,128)(2,1)}, bf16[32,1024]{1,0:T(8,128)(2,1)}) custom-call(bf16[64,128]{1,0:T(8,128)(2,1)} %get-tuple-element.9.dq_in, bf16[32,1024]{1,0:T(8,128)(2,1)} %get-tuple-element.10.dk_in, bf16[32,1024]{1,0:T(8,128)(2,1)} %get-tuple-element.11.dv_in), custom_call_target="tpu_custom_call" | custom-call | tf_op jit(solution)/shard_map/pallas_call | solution.py:421

commit v3 on v2

--- a/solution.py
+++ b/solution.py
@@ -19,7 +19,9 @@
 YS, ZS = 4, 8
 OWN_Q = OWN_ROWS * PER_GROUP
 SLOTS = 2 * ZS
-CHUNK = 2 * OWN_Q
+PER_CHUNK = 4
+CHUNK = PER_CHUNK * OWN_Q
+ROW = 2 * OWN_Q
 NQ = SLOTS * OWN_Q
 PIECE = 32
 PIECES = 16
@@ -218,30 +220,37 @@
     keys = kvbuf[:, 0].reshape(NT, DH)
     kt[...] = keys.T
 
-    def wait_pair(buf, ss, rs, c):
-        @pl.when(lax.rem(c, ZS // 2) > 0)
+    def wait_chunk(buf, ss, rs, c):
+        def wait(slot):
+            copy(buf.at[0], buf.at[slot], ss, rs, slot, sibling).wait_recv()
+
+        @pl.when(lax.rem(c, ZS // PER_CHUNK) > 0)
         def _():
-            copy(buf.at[0], buf.at[2 * c], ss, rs, 2 * c, sibling).wait_recv()
-
-        copy(buf.at[0], buf.at[2 * c + 1], ss, rs, 2 * c + 1, sibling).wait_recv()
+            wait(PER_CHUNK * c)
+
+        for i in range(1, PER_CHUNK):
+            wait(PER_CHUNK * c + i)
 
     def score_step(c, carry):
-        wait_pair(qbuf, q_ss, q_rs, c)
-        limit = jnp.where(c < ZS // 2, limits[0], limits[1])
-        queries = qbuf[pl.ds(2 * c, 2)].reshape(CHUNK, DH)
+        wait_chunk(qbuf, q_ss, q_rs, c)
+        limit = jnp.where(c < ZS // PER_CHUNK, limits[0], limits[1])
+        queries = qbuf[pl.ds(PER_CHUNK * c, PER_CHUNK)].reshape(CHUNK, DH)
         scores = lax.dot_general(
             kvbuf[:, 0].reshape(NT, DH), queries, NT_DIMS, preferred_element_type=F32
         ) * SCALE
-        scores = jnp.where(posbuf[...] < limit, scores, MASKED)
+        seen = posbuf[...] < limit
+        scores = jnp.where(jnp.concatenate([seen] * (CHUNK // DH), axis=1), scores, MASKED)
         peak = jnp.maximum(jnp.max(scores, axis=0, keepdims=True), FLOOR)
         terms = jnp.exp(scores - peak)
         total = jnp.sum(terms, axis=0, keepdims=True)
         ebuf[:, pl.ds(pl.multiple_of(c * CHUNK, CHUNK), CHUNK)] = terms.astype(BF16)
-        mrow[pl.ds(c, 1), :] = peak
-        lrow[pl.ds(c, 1), :] = total
+        for i in range(CHUNK // ROW):
+            row = pl.ds(CHUNK // ROW * c + i, 1)
+            mrow[row, :] = peak[:, i * ROW : (i + 1) * ROW]
+            lrow[row, :] = total[:, i * ROW : (i + 1) * ROW]
         return carry
 
-    lax.fori_loop(0, SLOTS // 2, score_step, 0)
+    lax.fori_loop(0, SLOTS // PER_CHUNK, score_step, 0)
 
     peaks = mrow[...]
     totals = lrow[...]
@@ -257,12 +266,12 @@
     lrow[...] = jnp.where(totals > 0.0, SCALE / jnp.maximum(totals, 1e-37), 0.0)
 
     def dscore_step(c, carry):
-        wait_pair(dobuf, do_ss, do_rs, c)
-        pair = dobuf[pl.ds(2 * c, 2)]
+        wait_chunk(dobuf, do_ss, do_rs, c)
+        pair = dobuf[pl.ds(PER_CHUNK * c, PER_CHUNK)]
         grads = pair[:, :OWN_Q].reshape(CHUNK, DH)
         parts = pair[:, OWN_Q:].astype(F32)
         dots_pair = parts[:, 0:1] + parts[:, 1:2] + parts[:, 2:3]
-        dots_row = jnp.concatenate([dots_pair[0, :, :OWN_Q], dots_pair[1, :, :OWN_Q]], axis=1)
+        dots_row = jnp.concatenate([dots_pair[i, :, :OWN_Q] for i in range(PER_CHUNK)], axis=1)
         dprob = lax.dot_general(
             kvbuf[:, 1].reshape(NT, DH), grads, NT_DIMS, preferred_element_type=F32
         )
@@ -270,11 +279,12 @@
         dscore = (ebuf[:, columns].astype(F32) * (dprob - dots_row)).astype(BF16)
         dsbuf[:, columns] = dscore
         dq_t = jnp.dot(kt[...], dscore, preferred_element_type=F32)
-        dq_t = dq_t * lrow[pl.ds(c, 1), :]
-        dqs[pl.ds(2 * c, 2)] = dq_t.T.astype(BF16).reshape(2, OWN_Q, DH)
+        shares = [lrow[pl.ds(CHUNK // ROW * c + i, 1), :] for i in range(CHUNK // ROW)]
+        dq_t = dq_t * jnp.concatenate(shares, axis=1)
+        dqs[pl.ds(PER_CHUNK * c, PER_CHUNK)] = dq_t.T.astype(BF16).reshape(PER_CHUNK, OWN_Q, DH)
         return carry
 
-    lax.fori_loop(0, SLOTS // 2, dscore_step, 0)
+    lax.fori_loop(0, SLOTS // PER_CHUNK, dscore_step, 0)
 
     for s in (0, ZS):
         for dz in range(1, ZS):
@@ -297,13 +307,13 @@
             fbuf[s + dz : s + dz + 1, :] = jnp.exp(mine - full_lse[row : row + 1])
     weight = jnp.exp(peaks - full_lse).T
     for c in range(SLOTS // 2):
-        rows = slice(c * CHUNK, (c + 1) * CHUNK)
+        rows = slice(c * ROW, (c + 1) * ROW)
         column = weight[:, c : c + 1]
         wq[rows] = (
-            qbuf[2 * c : 2 * c + 2].reshape(CHUNK, DH).astype(F32) * (column * SCALE)
+            qbuf[2 * c : 2 * c + 2].reshape(ROW, DH).astype(F32) * (column * SCALE)
         ).astype(BF16)
         wdo[rows] = (
-            dobuf[2 * c : 2 * c + 2, :OWN_Q].reshape(CHUNK, DH).astype(F32) * column
+            dobuf[2 * c : 2 * c + 2, :OWN_Q].reshape(ROW, DH).astype(F32) * column
         ).astype(BF16)
 
     half = PIECES * PIECE
@@ -325,10 +335,11 @@
             dkvs[i, pieces] = (
                 part.reshape(per, PIECE, DH) + sib_r[i, pieces].astype(F32)
             ).astype(BF16)
-
-    for p in range(1, PIECES):
-        send(dkvs.at[:, p], dkvr.at[p], out_ss, out_rs, p, piece_device(p))
-    dkvr[0] = dkvs[:, 0]
+        for p in range(1, PIECES):
+            send(
+                dkvs.at[i, p], dkvr.at[p, i], out_ss, out_rs, i * PIECES + p, piece_device(p)
+            )
+        dkvr[0, i] = dkvs[i, 0]
 
     shares = fbuf[...].T
 
@@ -345,8 +356,11 @@
     copy(dqy_s, dqy_r, dqy_ss, dqy_rs, 0, sibling).wait_recv()
     dq_out[...] = (grad + dqy_r[...]).astype(BF16)
 
-    for p in range(1, PIECES):
-        copy(dkvs.at[:, 0], dkvr.at[p], out_ss, out_rs, p, sibling).wait_recv()
+    for i in range(2):
+        for p in range(1, PIECES):
+            copy(
+                dkvs.at[i, 0], dkvr.at[p, i], out_ss, out_rs, i * PIECES + p, sibling
+            ).wait_recv()
     for d in range(HEADS):
         total = dkvr[d].astype(F32) + dkvr[HEADS + d].astype(F32)
         columns = pl.ds(pl.multiple_of(lax.rem(head + d, HEADS) * DH, DH), DH)
@@ -410,7 +424,7 @@
             pltpu.VMEM((PIECES, 2, PIECE, DH), BF16),
         ]
         + dma(SLOTS) + dma(SLOTS) + dma(PIECES) + dma(2) + dma(SLOTS) + dma(SLOTS)
-        + dma(1) + dma(2) + dma(PIECES),
+        + dma(1) + dma(2) + dma(2 * PIECES),
         compiler_params=pltpu.CompilerParams(
             collective_id=0, has_side_effects=True, vmem_limit_bytes=64 << 20
         ),

time: 52.2 us -> 51.1 us (0.979)
  Pallas kernels: 51.3 us -> 50.3 us
    pallas_call x1, Pallas kernels: 49.7 us -> 48.7 us  [shards(): pl.pallas_call(kernel, out_shape=out_shape, in_specs=[anywhere] * 8, out_...]
where the time goes in v3:
time: 51.1 us; the launch traced here: 50.9 us
  Pallas kernels  50.3 us (98%)
  between operations  0.64 us (1%)
    pallas_call x1, Pallas kernels, shards(): pl.pallas_call(kernel, out_shape=out_shape, in_specs=[anywhere] * 8, out_...  48.7 us
    pallas_call x1, Pallas kernels, shards(): pl.pallas_call(write_out, out_shape=out_shape, in_specs=[vmem] * 3, out_s...  1.57 us

profile of v3, /device:TPU:1, one launch (start us, length us, event | category | flops | bytes accessed | tf_op | source)
XLA Modules:
  0.0 50.9 jit_solution(9667265952195508389)
XLA Ops:
  0.6 48.7 %shard_map.103 = (bf16[64,128]{1,0:T(8,128)(2,1)}, bf16[32,1024]{1,0:T(8,128)(2,1)}, bf16[32,1024]{1,0:T(8,128)(2,1)}) custom-call(bf16[64,128]{1,0:T(8,128)(2,1)} %bitcast.20, bf16[64,128]{1,0:T(8,128)(2,1)} %bitcast.21, bf16[64,128]{1,0:T(8,128)(2,1)} %bitcast.22, f32[4,16]{1,0:T(4,128)} %lse_hbm.1, bf16[32,1024]{1,0:T(8,128)(2,1)} %k_hbm.1, ...), custom_call_target="tpu_custom_call" | custom-call | tf_op jit(solution)/shard_map/pallas_call | solution.py:390
  49.3 1.6 %shard_map.104 = (bf16[64,128]{1,0:T(8,128)(2,1)}, bf16[32,1024]{1,0:T(8,128)(2,1)}, bf16[32,1024]{1,0:T(8,128)(2,1)}) custom-call(bf16[64,128]{1,0:T(8,128)(2,1)} %get-tuple-element.9.dq_in, bf16[32,1024]{1,0:T(8,128)(2,1)} %get-tuple-element.10.dk_in, bf16[32,1024]{1,0:T(8,128)(2,1)} %get-tuple-element.11.dv_in), custom_call_target="tpu_custom_call" | custom-call | tf_op jit(solution)/shard_map/pallas_call | solution.py:435

commit v4 on v3

--- a/solution.py
+++ b/solution.py
@@ -69,9 +69,9 @@
     q_hbm, do_hbm, o_hbm, lse_hbm, k_hbm, v_hbm, len_hbm, end_hbm,
     dq_out, dk_out, dv_out,
     o_in, lse_in, k_in, v_in, len_in, end_in, in_sems,
-    qbuf, dobuf, kvs, kvbuf, lsebuf, mrow, lrow, posbuf, kt, ebuf, dsbuf, wq, wdo,
+    qbuf, dobuf, dotbuf, kvs, kvbuf, lsebuf, mrow, lrow, posbuf, kt, ebuf, dsbuf, wq, wdo,
     dqs, dqr, dqy_s, dqy_r, fbuf, sib_s, sib_r, dkvs, dkvr,
-    q_ss, q_rs, do_ss, do_rs, kv_ss, kv_rs, fwd_ss, fwd_rs, st_ss, st_rs, dq_ss, dq_rs, dqy_ss, dqy_rs,
+    q_ss, q_rs, do_ss, do_rs, dot_ss, dot_rs, kv_ss, kv_rs, fwd_ss, fwd_rs, st_ss, st_rs, dq_ss, dq_rs, dqy_ss, dqy_rs,
     sib_ss, sib_rs, out_ss, out_rs,
 ):
     ctx = lax.axis_index("ctx")
@@ -118,7 +118,7 @@
     arrivals = [
         pltpu.make_async_copy(src, dst, in_sems.at[i])
         for i, (src, dst) in enumerate((
-            (q_hbm, qbuf.at[0]), (do_hbm, dobuf.at[0, pl.ds(0, OWN_Q)]), (k_hbm, k_in),
+            (q_hbm, qbuf.at[0]), (do_hbm, dobuf.at[0]), (k_hbm, k_in),
             (v_hbm, v_in), (o_hbm, o_in), (lse_hbm, lse_in), (len_hbm, len_in),
             (end_hbm, end_in),
         ))
@@ -127,7 +127,7 @@
         arrival.start()
 
     barrier = pltpu.get_barrier_semaphore()
-    greeted = [row_device(s) for s in range(1, ZS + 1)]
+    greeted = [row_device(s) for s in (ZS, 4, 3, 5, 2, 6, 1, 7)]
     greeted += [user_device(p) for p in range(1, PIECES)]
     greeted += [
         device(y + jnp.where(low, 1, -1), z, core, jnp.where(low, 0, 4) + i) for i in range(4)
@@ -136,22 +136,6 @@
     for target in greeted:
         pl.semaphore_signal(barrier, inc=1, device_id=target, device_id_type=MESH)
 
-    for arrival in arrivals:
-        arrival.wait()
-    prod = dobuf[0, :OWN_Q].astype(F32) * o_in[...].astype(F32)
-    dots = jnp.sum(prod.T, axis=0, keepdims=True)
-    dots = jnp.concatenate([dots, jnp.zeros((1, DH - OWN_Q), F32)], axis=1)
-    high = dots.astype(BF16).astype(F32)
-    middle = (dots - high).astype(BF16).astype(F32)
-    rest = dots - high - middle
-    dobuf[0, OWN_Q:] = jnp.concatenate(
-        [high, middle, rest, jnp.zeros((13, DH), F32)], axis=0
-    ).astype(BF16)
-    for g in range(HEADS):
-        kvs[g, 0] = k_in[:, g * DH : (g + 1) * DH]
-        kvs[g, 1] = v_in[:, g * DH : (g + 1) * DH]
-    pl.semaphore_wait(barrier, len(greeted))
-
     def copy(src, dst, ss, rs, i, target):
         return pltpu.make_async_remote_copy(
             src_ref=src, dst_ref=dst, send_sem=ss.at[i], recv_sem=rs.at[i],
@@ -175,12 +159,28 @@
         for dz in range(1, ZS):
             send(buf.at[s], buf.at[s + ZS - dz], ss, rs, s + ZS - dz, row_device(dz))
 
+    q_arrival, do_arrival, k_arrival, v_arrival, *others = arrivals
+    q_arrival.wait()
+    pl.semaphore_wait(barrier, len(greeted))
     send(qbuf.at[0], qbuf.at[ZS], q_ss, q_rs, ZS, across)
-    send(dobuf.at[0], dobuf.at[ZS], do_ss, do_rs, ZS, across)
+    send_along(qbuf, q_ss, q_rs, 0)
+    k_arrival.wait()
+    v_arrival.wait()
+    for g in range(HEADS):
+        kvs[g, 0] = k_in[:, g * DH : (g + 1) * DH]
+        kvs[g, 1] = v_in[:, g * DH : (g + 1) * DH]
     for p in range(1, PIECES):
         send(*kv_copy(p))
-    send_along(qbuf, q_ss, q_rs, 0)
+    do_arrival.wait()
+    for arrival in others:
+        arrival.wait()
+    prod = dobuf[0].astype(F32) * o_in[...].astype(F32)
+    dots = jnp.sum(prod.T, axis=0, keepdims=True)
+    dotbuf[0] = jnp.concatenate([dots, jnp.zeros((1, DH - OWN_Q), F32)], axis=1)
+    send(dobuf.at[0], dobuf.at[ZS], do_ss, do_rs, ZS, across)
+    send(dotbuf.at[0], dotbuf.at[ZS], dot_ss, dot_rs, ZS, across)
     send_along(dobuf, do_ss, do_rs, 0)
+    send_along(dotbuf, dot_ss, dot_rs, 0)
 
     kvbuf[0, :, 0] = kvs[head]
 
@@ -210,6 +210,8 @@
     send_along(qbuf, q_ss, q_rs, ZS)
     copy(dobuf.at[0], dobuf.at[ZS], do_ss, do_rs, ZS, sibling).wait_recv()
     send_along(dobuf, do_ss, do_rs, ZS)
+    copy(dotbuf.at[0], dotbuf.at[ZS], dot_ss, dot_rs, ZS, sibling).wait_recv()
+    send_along(dotbuf, dot_ss, dot_rs, ZS)
 
     for p in range(1, PIECES):
         copy(*kv_copy(p)).wait_recv()
@@ -267,11 +269,10 @@
 
     def dscore_step(c, carry):
         wait_chunk(dobuf, do_ss, do_rs, c)
-        pair = dobuf[pl.ds(PER_CHUNK * c, PER_CHUNK)]
-        grads = pair[:, :OWN_Q].reshape(CHUNK, DH)
-        parts = pair[:, OWN_Q:].astype(F32)
-        dots_pair = parts[:, 0:1] + parts[:, 1:2] + parts[:, 2:3]
-        dots_row = jnp.concatenate([dots_pair[i, :, :OWN_Q] for i in range(PER_CHUNK)], axis=1)
+        wait_chunk(dotbuf, dot_ss, dot_rs, c)
+        grads = dobuf[pl.ds(PER_CHUNK * c, PER_CHUNK)].reshape(CHUNK, DH)
+        row = dotbuf[pl.ds(PER_CHUNK * c, PER_CHUNK)]
+        dots_row = jnp.concatenate([row[i, :, :OWN_Q] for i in range(PER_CHUNK)], axis=1)
         dprob = lax.dot_general(
             kvbuf[:, 1].reshape(NT, DH), grads, NT_DIMS, preferred_element_type=F32
         )
@@ -301,10 +302,6 @@
     top = functools.reduce(jnp.maximum, aligned)
     total = functools.reduce(jnp.add, [jnp.exp(part - top) for part in aligned])
     full_lse = top + jnp.log(total)
-    for dz in range(ZS):
-        for s, row in ((0, 0), (ZS, ZS // 2)):
-            mine = local_lse[row : row + 1] if dz == 0 else aligned[dz][row : row + 1]
-            fbuf[s + dz : s + dz + 1, :] = jnp.exp(mine - full_lse[row : row + 1])
     weight = jnp.exp(peaks - full_lse).T
     for c in range(SLOTS // 2):
         rows = slice(c * ROW, (c + 1) * ROW)
@@ -313,7 +310,7 @@
             qbuf[2 * c : 2 * c + 2].reshape(ROW, DH).astype(F32) * (column * SCALE)
         ).astype(BF16)
         wdo[rows] = (
-            dobuf[2 * c : 2 * c + 2, :OWN_Q].reshape(ROW, DH).astype(F32) * column
+            dobuf[2 * c : 2 * c + 2].reshape(ROW, DH).astype(F32) * column
         ).astype(BF16)
 
     half = PIECES * PIECE
@@ -341,6 +338,10 @@
             )
         dkvr[0, i] = dkvs[i, 0]
 
+    for dz in range(ZS):
+        for s, row in ((0, 0), (ZS, ZS // 2)):
+            mine = local_lse[row : row + 1] if dz == 0 else aligned[dz][row : row + 1]
+            fbuf[s + dz : s + dz + 1, :] = jnp.exp(mine - full_lse[row : row + 1])
     shares = fbuf[...].T
 
     def summed(s):
@@ -401,7 +402,8 @@
             pltpu.SMEM((YS,), jnp.int32),
             pltpu.SemaphoreType.DMA((8,)),
             pltpu.VMEM((SLOTS, OWN_Q, DH), BF16),
-            pltpu.VMEM((SLOTS, OWN_Q + 16, DH), BF16),
+            pltpu.VMEM((SLOTS, OWN_Q, DH), BF16),
+            pltpu.VMEM((SLOTS, 1, DH), F32),
             pltpu.VMEM((HEADS, 2, PIECE, DH), BF16),
             pltpu.VMEM((2, 2, PIECES, PIECE, DH), BF16),
             pltpu.VMEM((SLOTS, ZS, DH), F32),
@@ -423,7 +425,7 @@
             pltpu.VMEM((2, PIECES, PIECE, DH), BF16),
             pltpu.VMEM((PIECES, 2, PIECE, DH), BF16),
         ]
-        + dma(SLOTS) + dma(SLOTS) + dma(PIECES) + dma(2) + dma(SLOTS) + dma(SLOTS)
+        + dma(SLOTS) + dma(SLOTS) + dma(SLOTS) + dma(PIECES) + dma(2) + dma(SLOTS) + dma(SLOTS)
         + dma(1) + dma(2) + dma(2 * PIECES),
         compiler_params=pltpu.CompilerParams(
             collective_id=0, has_side_effects=True, vmem_limit_bytes=64 << 20

time: 51.1 us -> 51.2 us (level)
  no operation moved by 1% of the time
where the time goes in v4:
time: 51.2 us; the launch traced here: 51 us
  Pallas kernels  50.3 us (98%)
  between operations  0.64 us (1%)
    pallas_call x1, Pallas kernels, shards(): pl.pallas_call(kernel, out_shape=out_shape, in_specs=[anywhere] * 8, out_...  48.8 us
    pallas_call x1, Pallas kernels, shards(): pl.pallas_call(write_out, out_shape=out_shape, in_specs=[vmem] * 3, out_s...  1.57 us

profile of v4, /device:TPU:1, one launch (start us, length us, event | category | flops | bytes accessed | tf_op | source)
XLA Modules:
  0.0 51.0 jit_solution(17136000860421202302)
XLA Ops:
  0.6 48.8 %shard_map.103 = (bf16[64,128]{1,0:T(8,128)(2,1)}, bf16[32,1024]{1,0:T(8,128)(2,1)}, bf16[32,1024]{1,0:T(8,128)(2,1)}) custom-call(bf16[64,128]{1,0:T(8,128)(2,1)} %bitcast.20, bf16[64,128]{1,0:T(8,128)(2,1)} %bitcast.21, bf16[64,128]{1,0:T(8,128)(2,1)} %bitcast.22, f32[4,16]{1,0:T(4,128)} %lse_hbm.1, bf16[32,1024]{1,0:T(8,128)(2,1)} %k_hbm.1, ...), custom_call_target="tpu_custom_call" | custom-call | tf_op jit(solution)/shard_map/pallas_call | solution.py:391
  49.4 1.6 %shard_map.104 = (bf16[64,128]{1,0:T(8,128)(2,1)}, bf16[32,1024]{1,0:T(8,128)(2,1)}, bf16[32,1024]{1,0:T(8,128)(2,1)}) custom-call(bf16[64,128]{1,0:T(8,128)(2,1)} %get-tuple-element.9.dq_in, bf16[32,1024]{1,0:T(8,128)(2,1)} %get-tuple-element.10.dk_in, bf16[32,1024]{1,0:T(8,128)(2,1)} %get-tuple-element.11.dv_in), custom_call_target="tpu_custom_call" | custom-call | tf_op jit(solution)/shard_map/pallas_call | solution.py:437
